TPU v7x, 512 devices: a whole 4x8x8 slice. The times are simulated.
512 devices in a mesh: row: 16 (over y, x_hi), col: 32 (over z, x_lo, core).
Axes of the slice: x: 4 (x_hi: 2, x_lo: 2; x = x_hi * 2 + x_lo), y: 8, z: 8, core: 2. Of those that a mesh axis runs over, the one named last changes fastest.
Arguments:
- matrix: float32 [12288, 12288], P('row', 'col'), may hold values from -24 to 24
- vectors: float32 [12288, 12288], P('row', 'col'), may hold values from -6 to 6
- rotations: float32 [16, 768, 768], P('row', 'col'), may hold values from -0.21875 to 0.21875
Outputs:
- new_matrix: float32 [12288, 12288], P('row', 'col')
- new_vectors: float32 [12288, 12288], P('row', 'col')
All inputs are finite; a program needn't handle non-finite values.
Results may differ from a plain program's by a relative error of at most 0.000096.
Values sent between devices are 32-bit elements; how exact they have to be, the bound alone decides.
A program may use at most 64 MiB of HBM per device.

v0:
```python
import jax
import jax.numpy as jnp
from jax import lax
from jax.sharding import PartitionSpec as P


def passed_along(value, axis, steps):
    count = lax.axis_size(axis)
    first, last = (max(0, -steps), min(count, count - steps))
    return lax.ppermute(value, axis, [(source, source + steps) for source in range(first, last)])


def broadcast(value, axis, source):
    kept = jnp.where(lax.axis_index(axis) == source, value, 0).astype(value.dtype)
    return lax.psum(kept, axis)


def from_partner(value, axis, stride):
    return lax.ppermute(value, axis, [(i, i ^ 1 << stride) for i in range(lax.axis_size(axis))])


def mix_blocks(mine, other, col_rot, slot, width, out_start):
    high = lax.Precision.HIGHEST
    columns = lax.dynamic_slice_in_dim(col_rot, out_start, width, 1)
    own_rows = lax.dynamic_slice_in_dim(columns, slot * width, width, 0)
    other_rows = lax.dynamic_slice_in_dim(columns, (1 - slot) * width, width, 0)
    first = jnp.einsum(
        "srk,kb->srb", mine, own_rows, precision=high, preferred_element_type=jnp.float32
    )
    second = jnp.einsum(
        "srk,kb->srb", other, other_rows, precision=high, preferred_element_type=jnp.float32
    )
    return first + second


def move_columns(plans):
    moved = []
    for payload, distance in plans:
        moved.append(passed_along(payload, "col", distance))
    return moved


def move_rows(plans):
    moved = []
    for payload, distance in plans:
        moved.append(passed_along(payload, "row", distance))
    return moved


def on_device(matrix, vectors, rotations):
    width = matrix.shape[1]
    row_pos = lax.axis_index("row")
    col_pos = lax.axis_index("col")
    last_row = lax.axis_size("row") - 1
    last_col = lax.axis_size("col") - 1
    slot = col_pos % 2
    high = lax.Precision.HIGHEST
    pair_rot = lax.all_gather(rotations[0], "col", axis=0, tiled=True)
    left = lax.dot_general(
        pair_rot,
        matrix,
        (((0,), (0,)), ((), ())),
        precision=high,
        preferred_element_type=jnp.float32,
    )
    col_rot = broadcast(pair_rot, "row", col_pos // 2)
    mine = jnp.stack([left, vectors])
    other = from_partner(mine, "col", 0)
    own_new = mix_blocks(mine, other, col_rot, slot, width, slot * width)
    other_new = mix_blocks(mine, other, col_rot, slot, width, (1 - slot) * width)
    forward, backward = move_columns(
        [(jnp.where(col_pos == 0, other_new, own_new), 2), (own_new, -2)]
    )
    placed = jnp.where(slot == 0, forward, backward)
    placed = jnp.where(col_pos == last_col, other_new, placed)
    placed = jnp.where(col_pos == 0, own_new, placed)
    tile = placed[0]
    upper = tile[:width]
    lower = tile[width:]
    from_above, from_below = move_rows([(jnp.where(row_pos == 0, lower, upper), 1), (lower, -1)])
    new_upper = jnp.where(row_pos == 0, upper, from_above)
    new_lower = jnp.where(row_pos == last_row, upper, from_below)
    return (jnp.concatenate([new_upper, new_lower], axis=0), placed[1])


def solution(mesh):
    in_specs = (P("row", "col"), P("row", "col"), P("row", "col", None))
    out_specs = (P("row", "col"), P("row", "col"))
    return jax.shard_map(
        on_device, mesh=mesh, in_specs=in_specs, out_specs=out_specs, check_vma=False
    )
```

profile of v0, /device:TPU:73, one launch (start us, length us, event | category | flops | bytes accessed | tf_op | source)
XLA Modules:
  0.0 427.3 jit_solution(11919965808834036603)
XLA Ops:
  7.2 0.0 copy-start
  7.2 0.0 all-gather.3.cloned.1.call-start
  7.2 0.7 all-gather.3.cloned.1.call-update
  7.9 0.0 all-reduce.2.cloned.1.call-start
  8.0 73.8 %all-gather.3.cloned.1.call-done = f32[1,768,768]{2,1,0:T(8,128)} async-done(((f32[1,24,768]{2,1,0:T(8,128)}), f32[1,768,768]{2,1,0:T(8,128)}) %all-gather.3.cloned.1.call-update) | async-done | bytes 2359312 | tf_op jit(solution)/shard_map/all_gather | solution.py:58
  81.8 3.3 bitcast_select_fusion
  85.1 0.0 all-reduce.2.cloned.1.call-update
  85.1 0.0 copy-done
  85.1 0.0 copy-start.2
  85.1 5.6 %fusion.2 = f32[1,768,384]{2,1,0:T(8,128)S(1)} fusion(f32[768,384]{1,0:T(8,128)S(1)} %copy-done, f32[1,768,768]{2,1,0:T(8,128)} %all-gather.3.cloned.1.call-done), kind=kOutput, calls=%fused_computation.7 | convolution fusion | flops 2717908992 | bytes 4718592 | tf_op jit(solution)/shard_map/dot_general | solution.py:59
  90.7 0.0 copy-done.2
  90.7 1.6 pad_maximum_fusion
  92.4 2.4 collective-permute-start
  94.8 155.0 %all-reduce.2.cloned.1.call-done = f32[768,768]{1,0:T(8,128)} async-done(((f32[768,768]{1,0:T(8,128)}), f32[768,768]{1,0:T(8,128)}) %all-reduce.2.cloned.1.call-update) | async-done | bytes 2359312 | tf_op jit(solution)/shard_map/psum | solution.py:15
  249.8 0.0 copy-start.3
  249.8 6.3 %fusion.9 = f32[2,768,384]{2,1,0:T(8,128)S(1)} fusion(f32[768,768]{1,0:T(8,128)} %all-reduce.2.cloned.1.call-done, s32[]{:T(128)S(6)} %select_n.82, f32[1,768,384]{2,1,0:T(8,128)S(1)} %bitcast.41, f32[1,768,384]{2,1,0:T(8,128)S(1)} %fusion.2), kind=kOutput, calls=%fused_computation.17 | convolution fusion | flops 2718498816 | bytes 5308420 | tf_op jit(solution)/shard_map/srk,kb->srb/dot_general | solution.py:27
  256.1 0.0 copy-done.3
  256.1 5.0 %fusion.6 = f32[2,768,384]{2,1,0:T(8,128)S(1)} fusion(f32[768,768]{1,0:T(8,128)S(1)} %copy-done.3, s32[]{:T(128)S(6)} %select_n.82, s32[]{:T(128)S(6)} %select_n.84, f32[1,768,384]{2,1,0:T(8,128)S(1)} %bitcast.42, f32[1,768,384]{2,1,0:T(8,128)S(1)} %fusion.2), kind=kOutput, calls=%fused_computation.14 | convolution fusion | flops 2718498816 | bytes 5308424 | tf_op jit(solution)/shard_map/srk,kb->srb/dot_general | solution.py:27
  261.2 0.0 collective-permute-done
  261.2 6.7 %convolution_add_fusion.1 = f32[2,768,384]{2,1,0:T(8,128)S(1)} fusion(f32[2,768,384]{2,1,0:T(8,128)S(1)} %fusion.9, f32[2,768,384]{2,1,0:T(8,128)} %collective-permute-done, f32[768,768]{1,0:T(8,128)S(1)} %copy-done.3, s32[]{:T(128)S(6)} %select_n.84, s32[]{:T(128)S(6)} %select_n.82), kind=kOutput, calls=%fused_computation.6 | convolution fusion | flops 2718498816 | bytes 7667720 | tf_op jit(solution)/shard_map/srk,kb->srb/dot_general | solution.py:30
  267.8 7.7 %broadcast_select_fusion = (f32[2,768,384]{2,1,0:T(8,128)}, f32[2,768,384]{2,1,0:T(8,128)}) fusion(f32[2,768,384]{2,1,0:T(8,128)S(1)} %convolution_add_fusion.1, pred[]{:T(512)S(6)} %eq.23, f32[2,768,384]{2,1,0:T(8,128)S(1)} %fusion.6, f32[2,768,384]{2,1,0:T(8,128)} %collective-permute-done, f32[768,768]{1,0:T(8,128)S(1)} %copy-done.3, s32[]{:T(128)S(6)} %select_n.84), kind=kOutput, calls=%fused_computation.10 | convolution fusion | flops 2719088640 | bytes 12386309 | tf_op jit(solution)/shard_map/srk,kb->srb/dot_general | solution.py:30
  275.6 2.1 collective-permute-start.1
  277.7 4.1 collective-permute-start.2
  281.8 93.0 %collective-permute-done.1 = f32[2,768,384]{2,1,0:T(8,128)} collective-permute-done((f32[2,768,384]{2,1,0:T(8,128)}, f32[2,768,384]{2,1,0:T(8,128)}, u32[]{:S(2)}, u32[]{:S(2)}) %collective-permute-start.1) | collective-permute-done | bytes 2359328 | tf_op jit(solution)/shard_map/ppermute | solution.py:10
  374.7 7.7 %collective-permute-done.2 = f32[2,768,384]{2,1,0:T(8,128)} collective-permute-done((f32[2,768,384]{2,1,0:T(8,128)S(1)}, f32[2,768,384]{2,1,0:T(8,128)}, u32[]{:S(2)}, u32[]{:S(2)}) %collective-permute-start.2) | collective-permute-done | bytes 2359328 | tf_op jit(solution)/shard_map/ppermute | solution.py:10
  382.4 2.1 select_select_fusion
  384.5 0.0 copy-start.1
  384.5 1.4 copy-done.1
  385.9 0.1 fusion.17
  386.0 4.8 %collective-permute-start.3 = (f32[384,384]{1,0:T(8,128)S(1)}, f32[384,384]{1,0:T(8,128)S(1)}, u32[]{:S(2)}, u32[]{:S(2)}) collective-permute-start(f32[384,384]{1,0:T(8,128)S(1)} %fusion.17), channel_id=1, source_target_pairs={{0,32},{32,64},{64,96},{96,128},{128,160},{160,192},{192,224},{224... | collective-permute-start | bytes 1769480 | tf_op jit(solution)/shard_map/ppermute | solution.py:10
  390.8 2.9 collective-permute-start.4
  393.7 2.4 slice_bitcast_fusion
  396.0 19.5 %collective-permute-done.3 = f32[384,384]{1,0:T(8,128)S(1)} collective-permute-done((f32[384,384]{1,0:T(8,128)S(1)}, f32[384,384]{1,0:T(8,128)S(1)}, u32[]{:S(2)}, u32[]{:S(2)}) %collective-permute-start.3) | collective-permute-done | bytes 589856 | tf_op jit(solution)/shard_map/ppermute | solution.py:10
  415.6 2.6 collective-permute-done.4
  418.2 1.2 fusion.16
  419.3 1.1 pad_maximum_fusion.1
  (1 shorter events, 0.0 us)
Async XLA Ops:
  7.2 77.9 %copy-start = (f32[768,384]{1,0:T(8,128)S(1)}, f32[768,384]{1,0:T(8,128)}, u32[]{:S(2)}) copy-start(f32[768,384]{1,0:T(8,128)} %param.3) | copy-start | bytes 3538948
  7.2 74.6 %all-gather.3.cloned.1.call-start = ((), (), s32[]{:S(2)}) async-start(), calls=%async_computation.1 | async-start | bytes 2433024 | tf_op jit(solution)/shard_map/all_gather | solution.py:58
  7.9 241.9 %all-reduce.2.cloned.1.call-start = ((), (), s32[]{:S(2)}) async-start(), calls=%async_computation | async-start | bytes 4718592 | tf_op jit(solution)/shard_map/psum | solution.py:15
  85.1 5.6 %copy-start.2 = (f32[768,384]{1,0:T(8,128)S(1)}, f32[768,384]{1,0:T(8,128)}, u32[]{:S(2)}) copy-start(f32[768,384]{1,0:T(8,128)} %param.4) | copy-start | bytes 3538948
  92.4 168.8 %collective-permute-start = (f32[2,768,384]{2,1,0:T(8,128)}, f32[2,768,384]{2,1,0:T(8,128)}, u32[]{:S(2)}, u32[]{:S(2)}) collective-permute-start(f32[2,768,384]{2,1,0:T(8,128)} %pad_maximum_fusion), channel_id=1, source_target_pairs={{0,1},{1,0},{2,3},{3,2},{4,5},{5,4},{6,7},{7,6},{8,9},{9,8},{10,11... | collective-permute-start | bytes 7077896 | tf_op jit(solution)/shard_map/ppermute | solution.py:19
  249.8 6.3 %copy-start.3 = (f32[768,768]{1,0:T(8,128)S(1)}, f32[768,768]{1,0:T(8,128)}, u32[]{:S(2)}) copy-start(f32[768,768]{1,0:T(8,128)} %all-reduce.2.cloned.1.call-done) | copy-start | bytes 7077892
  275.6 99.2 %collective-permute-start.1 = (f32[2,768,384]{2,1,0:T(8,128)}, f32[2,768,384]{2,1,0:T(8,128)}, u32[]{:S(2)}, u32[]{:S(2)}) collective-permute-start(f32[2,768,384]{2,1,0:T(8,128)} %get-tuple-element.4), channel_id=1, source_target_pairs={{0,2},{1,3},{2,4},{3,5},{4,6},{5,7},{6,8},{7,9},{8,10},{9,11},{10,... | collective-permute-start | bytes 7077896 | tf_op jit(solution)/shard_map/ppermute | solution.py:10
  277.7 104.7 %collective-permute-start.2 = (f32[2,768,384]{2,1,0:T(8,128)S(1)}, f32[2,768,384]{2,1,0:T(8,128)}, u32[]{:S(2)}, u32[]{:S(2)}) collective-permute-start(f32[2,768,384]{2,1,0:T(8,128)S(1)} %convolution_add_fusion.1), channel_id=1, source_target_pairs={{2,0},{3,1},{4,2},{5,3},{6,4},{7,5},{8,6},{9,7},{10,8},{11,9},{12,... | collective-permute-start | bytes 7077896 | tf_op jit(solution)/shard_map/ppermute | solution.py:10
  384.5 1.4 copy-start.1
  386.0 29.6 %collective-permute-start.3 = (f32[384,384]{1,0:T(8,128)S(1)}, f32[384,384]{1,0:T(8,128)S(1)}, u32[]{:S(2)}, u32[]{:S(2)}) collective-permute-start(f32[384,384]{1,0:T(8,128)S(1)} %fusion.17), channel_id=1, source_target_pairs={{0,32},{32,64},{64,96},{96,128},{128,160},{160,192},{192,224},{224... | collective-permute-start | bytes 1769480 | tf_op jit(solution)/shard_map/ppermute | solution.py:10
  390.8 27.4 %collective-permute-start.4 = (f32[384,384]{1,0:T(8,128)S(1)}, f32[384,384]{1,0:T(8,128)S(1)}, u32[]{:S(2)}, u32[]{:S(2)}) collective-permute-start(f32[384,384]{1,0:T(8,128)S(1)} %slice_bitcast_fusion.1), channel_id=1, source_target_pairs={{32,0},{64,32},{96,64},{128,96},{160,128},{192,160},{224,192},{256... | collective-permute-start | bytes 1769480 | tf_op jit(solution)/shard_map/ppermute | solution.py:10
Sparse Core Ops, SparseCore 0:
  10.2 71.6 all-gather.2
  85.2 164.5 all-reduce.1
where the time goes:
time: 428 us; the launch traced here: 427 us
  waiting for transfers between devices  352 us (82%)
  matrix products  31.3 us (7%)
  starting transfers between devices  16.3 us (4%)
  between operations  14.3 us (3%)
  other arithmetic  9.29 us (2%)
    psum x1, waiting for transfers between devices, broadcast(): return lax.psum(kept, axis)  155 us
    ppermute x4, waiting for transfers between devices, passed_along(): lax.ppermute(value, axis, [(source, source + steps) for source in range(f...  123 us
    all_gather x1, waiting for transfers between devices, on_device(): pair_rot = lax.all_gather(rotations[0], 'col', axis=0, tiled=True)  73.8 us
    dot_general x2, matrix products, mix_blocks(): jnp.einsum('srk,kb->srb', other, other_rows, precision=high, preferred_el...  14.4 us
    ppermute x4, starting transfers between devices, passed_along(): lax.ppermute(value, axis, [(source, source + steps) for source in range(f...  13.9 us
    dot_general x2, matrix products, mix_blocks(): jnp.einsum('srk,kb->srb', mine, own_rows, precision=high, preferred_eleme...  11.3 us
  transfers between devices with their start and end apart: 7, of which 6 were waited for; matrix products, arithmetic and copies ran while one was open for 5% of the time, Pallas kernels for 0%

commit v1 on v0

v1 whole, which is shorter than its diff:
```python
import functools

import jax
import jax.numpy as jnp
from jax import lax
from jax.experimental import pallas as pl
from jax.experimental.pallas import tpu as pltpu
from jax.sharding import PartitionSpec as P

MESH = pl.DeviceIdType.MESH
F32 = jnp.float32
BF16 = jnp.bfloat16


def target(k, count):
    moved = jnp.where(lax.rem(k, 2) == 0, k + 2, k - 2)
    moved = jnp.where(k == count - 2, count - 1, moved)
    moved = jnp.where(k == 1, 2, moved)
    return jnp.where(k == 0, 0, moved)


def origin(k, count):
    moved = jnp.where(lax.rem(k, 2) == 0, k - 2, k + 2)
    moved = jnp.where(k == count - 1, count - 2, moved)
    moved = jnp.where(k == 2, 1, moved)
    return jnp.where(k == 0, 0, moved)


def halves(value):
    high = value.astype(BF16)
    return high, (value - high.astype(F32)).astype(BF16)


def product(a, b, contract):
    dims = ((contract, (0,)), ((), ()))
    dot = functools.partial(lax.dot_general, dimension_numbers=dims, preferred_element_type=F32)
    return dot(a[0], b[0]) + (dot(a[0], b[1]) + dot(a[1], b[0]))


def kernel(n_row, n_col, m_ref, v_ref, rot_ref, om_ref, ov_ref, mf, vf, rp, rr, rph, rpl, mrh, mrl,
           out_v, out_m, send_sem, recv_sem, loc_sem):
    height, width = m_ref.shape
    full = 2 * width
    shard = rot_ref.shape[1]
    n_y, n_z = n_row // 2, n_col // 4
    r, c = lax.axis_index("row"), lax.axis_index("col")
    y, h = lax.div(r, 2), lax.rem(r, 2)
    p, s = lax.div(c, 2), lax.rem(c, 2)
    z, l = lax.div(p, 2), lax.rem(p, 2)
    core, lane = (r, c + 1 - 2 * s), (r, c + 2 - 4 * l)
    z_next, z_last = (r, lax.rem(c + 4, n_col)), (r, lax.rem(c + n_col - 4, n_col))
    half_row = (r + 1 - 2 * h, c)
    y_next, y_last = (lax.rem(r + 2, n_row), c), (lax.rem(r + n_row - 2, n_row), c)
    across = [(p, 2 * r + t) for t in range(2)]
    across_self = [(p == r) & (s == t) for t in range(2)]
    col_to, col_from = target(c, n_col), origin(c, n_col)
    row_to = [target(2 * r + u, 2 * n_row) for u in range(2)]
    row_from = [origin(2 * r + u, 2 * n_row) for u in range(2)]
    v_to, v_from = (r, col_to), (r, col_from)
    v_self = col_to == c
    m_to = [(lax.div(row_to[u], 2), col_to) for u in range(2)]
    m_from = [(lax.div(row_from[u], 2), col_from) for u in range(2)]
    m_self = [(m_to[u][0] == r) & (col_to == c) for u in range(2)]
    m_same = [(m_from[u][0] == r) & (col_from == c) for u in range(2)]

    barrier = pltpu.get_barrier_semaphore()
    awaited = 7

    def greet(device):
        pl.semaphore_signal(barrier, inc=1, device_id=device, device_id_type=MESH)

    for device in (core, lane, z_next, z_last, half_row, y_next, y_last):
        greet(device)
    for same in (*across_self, v_self, *m_self):
        awaited = awaited + jnp.where(same, 0, 1)
    for device, same in ((across[0], across_self[0]), (across[1], across_self[1]), (v_from, v_self),
                         (m_from[0], m_same[0]), (m_from[1], m_same[1])):
        pl.when(jnp.logical_not(same))(functools.partial(greet, device))

    own = pltpu.make_async_copy(rot_ref.at[0], rr.at[z, l, s], loc_sem.at[0])
    own.start()
    own_m = pltpu.make_async_copy(m_ref, mf.at[:, pl.ds(pl.multiple_of(s * width, width), width)], loc_sem.at[1])
    own_v = pltpu.make_async_copy(v_ref, vf.at[:, pl.ds(pl.multiple_of(s * width, width), width)], loc_sem.at[2])
    own_m.start()
    own_v.start()
    pl.semaphore_wait(barrier, awaited)

    index = iter(range(200))
    sends = []

    def describe(src, dst, device, sem=None):
        sem = next(index) if sem is None else sem
        return pltpu.make_async_remote_copy(
            src_ref=src, dst_ref=dst, send_sem=send_sem.at[sem], recv_sem=recv_sem.at[sem],
            device_id=device, device_id_type=MESH)

    def send(src, dst, device):
        copy = describe(src, dst, device)
        copy.start()
        sends.append(copy)
        return copy

    crossed = []
    for t in range(2):
        src = rot_ref.at[0, :, t * width:(t + 1) * width]
        sem = next(index)
        far = describe(src, rp.at[c], across[t], sem)
        near = pltpu.make_async_copy(src, rp.at[c], recv_sem.at[sem])
        pl.when(jnp.logical_not(across_self[t]))(far.start)
        pl.when(across_self[t])(near.start)
        crossed.append((far, across_self[t], t, sem))
    src = rot_ref.at[0]
    ring_z = {(0, 1, 0): send(src, rr.at[z, l, s], z_next), (0, -1, 0): send(src, rr.at[z, l, s], z_last)}
    to_lane = send(src, rr.at[z, l, s], lane)
    mine = pl.ds(pl.multiple_of(s * width, width), width)
    got_v = send(v_ref, vf.at[:, mine], core)
    got_m = send(m_ref, mf.at[:, mine], core)

    def row_block(who_y, who_h):
        return rp.at[pl.ds(2 * (2 * who_y + who_h), 2)]

    def chip_block(who_z, who_l):
        return rr.at[who_z, who_l, s]

    for t in range(2):
        far, _, _, sem = crossed[t]
        pl.when(s == t)(lambda sem=sem: pltpu.make_async_copy(
            rp.at[pl.ds(2 * r, 2)], rp.at[pl.ds(2 * r, 2)], recv_sem.at[sem]).wait())
    block = row_block(y, h)
    ring_y = {(0, 1, 0): send(block, block, y_next), (0, -1, 0): send(block, block, y_last)}
    to_half = send(block, block, half_row)

    to_lane.wait_recv()
    for d, device in ((1, z_next), (-1, z_last)):
        ring_z[0, d, 1] = send(chip_block(z, 1 - l), chip_block(z, 1 - l), device)
    own.wait()
    both = rr.at[z, :, s]
    core_z = [send(both, both, core)]
    to_half.wait_recv()
    block = row_block(y, 1 - h)
    for d, device in ((1, y_next), (-1, y_last)):
        ring_y[0, d, 1] = send(block, block, device)

    def ring(k, size, ring_of, place, pick, ways):
        far = size // 2
        for lane_of in range(2):
            for d, device in ways:
                if (k - 1, d, lane_of) not in ring_of:
                    continue
                ring_of[k - 1, d, lane_of].wait_recv()
                at = lax.rem(place - d * k + size, size)
                block = pick(at, lane_of)
                if k < far - 1 or (k == far - 1 and (d == 1) == (lane_of == 0)):
                    ring_of[k, d, lane_of] = send(block, block, device)

    pick_y = lambda at, lane_of: row_block(at, h if lane_of == 0 else 1 - h)
    pick_z = lambda at, lane_of: chip_block(at, l if lane_of == 0 else 1 - l)
    ways_y, ways_z = ((1, y_next), (-1, y_last)), ((1, z_next), (-1, z_last))
    for k in range(1, max(n_y, n_z) // 2 + 1):
        if k <= n_y // 2:
            ring(k, n_y, ring_y, y, pick_y, ways_y)
        if k <= n_z // 2:
            ring(k, n_z, ring_z, z, pick_z, ways_z)
            for d in (1, -1) if k < n_z // 2 else (1,):
                both = rr.at[lax.rem(z - d * k + n_z, n_z), :, s]
                core_z.append(send(both, both, core))
    own_v.wait()
    own_m.wait()
    got_v.wait_recv()
    got_m.wait_recv()

    count = n_col // 4
    rows_of = 4 * shard

    @pl.loop(0, count)
    def _(i):
        high, low = halves(rp[pl.ds(4 * i, 4)].reshape(rows_of, width))
        at = pl.ds(pl.multiple_of(i * rows_of, rows_of), rows_of)
        rph[at, :] = high
        rpl[at, :] = low

    step = 256 if height % 256 == 0 else height // 3
    v_sem = next(index)
    m_sem = [next(index) for _ in range(2)]

    def move(src, dst, device, same, sem):
        far = describe(src, dst, device, sem)
        pl.when(jnp.logical_not(same))(far.start)
        pl.when(same)(pltpu.make_async_copy(src, dst, recv_sem.at[sem]).start)

    @pl.loop(0, height // step)
    def _(i):
        at = pl.ds(pl.multiple_of(i * step, step), step)
        out_v[at, :] = product(halves(vf[at, :]), (rph[...], rpl[...]), (1,))
        move(out_v.at[at], ov_ref.at[at], v_to, v_self, v_sem)

    @pl.loop(0, height // step)
    def _(i):
        at = pl.ds(pl.multiple_of(i * step, step), step)
        high, low = halves(product(halves(mf[at, :]), (rph[...], rpl[...]), (1,)))
        mrh[at, :] = high
        mrl[at, :] = low

    for copy in core_z:
        copy.wait_recv()

    tile = 128 if width % 128 == 0 else width
    for u in range(2):
        slot = lax.rem(row_to[u], 2)
        dst_base = slot * width
        sem = jnp.where(slot == 0, m_sem[0], m_sem[1])

        @pl.loop(0, width // tile)
        def _(i):
            src_at = pl.multiple_of(u * width + i * tile, tile)
            part = rr[:, :, :, :, pl.ds(src_at, tile)].reshape(height, tile)
            at = pl.ds(src_at, tile)
            out_m[at, :] = product(halves(part), (mrh[...], mrl[...]), (0,))
            to = pl.ds(pl.multiple_of(dst_base + i * tile, tile), tile)
            move(out_m.at[at], om_ref.at[to], m_to[u], m_self[u], sem)

    pltpu.make_async_copy(ov_ref, ov_ref, recv_sem.at[v_sem]).wait()
    for u in range(2):
        part = om_ref.at[u * width:(u + 1) * width]
        pltpu.make_async_copy(part, part, recv_sem.at[m_sem[u]]).wait()
    for copy in sends:
        copy.wait_send()
    for far, same, _, _ in crossed:
        pl.when(jnp.logical_not(same))(far.wait_send)
    v_out = describe(out_v, ov_ref, v_to, v_sem)
    pl.when(jnp.logical_not(v_self))(v_out.wait_send)
    for u in range(2):
        slot = lax.rem(row_to[u], 2)
        sem = jnp.where(slot == 0, m_sem[0], m_sem[1])
        part = out_m.at[u * width:(u + 1) * width]
        out = describe(part, om_ref.at[0:width], m_to[u], sem)
        pl.when(jnp.logical_not(m_self[u]))(out.wait_send)


def solution(mesh):
    n_row, n_col = mesh.shape["row"], mesh.shape["col"]

    def on_device(matrix, vectors, rotations):
        height, width = matrix.shape
        shard = rotations.shape[1]
        any_space = pl.BlockSpec(memory_space=pl.ANY)
        return pl.pallas_call(
            functools.partial(kernel, n_row, n_col),
            out_shape=[jax.ShapeDtypeStruct((height, width), F32)] * 2,
            in_specs=[any_space] * 3,
            out_specs=[any_space] * 2,
            scratch_shapes=[
                pltpu.VMEM((height, 2 * width), F32),
                pltpu.VMEM((height, 2 * width), F32),
                pltpu.VMEM((n_col, shard, width), F32),
                pltpu.VMEM((n_col // 4, 2, 2, shard, 2 * width), F32),
                pltpu.VMEM((height, width), BF16),
                pltpu.VMEM((height, width), BF16),
                pltpu.VMEM((height, width), BF16),
                pltpu.VMEM((height, width), BF16),
                pltpu.VMEM((height, width), F32),
                pltpu.VMEM((height, width), F32),
                pltpu.SemaphoreType.DMA((64,)),
                pltpu.SemaphoreType.DMA((64,)),
                pltpu.SemaphoreType.DMA((3,)),
            ],
            compiler_params=pltpu.CompilerParams(
                collective_id=0, has_side_effects=True, vmem_limit_bytes=40 * 1024 * 1024),
            name="round",
        )(matrix, vectors, rotations)

    return jax.shard_map(
        on_device, mesh=mesh,
        in_specs=(P("row", "col"), P("row", "col"), P("row", "col", None)),
        out_specs=(P("row", "col"), P("row", "col")), check_vma=False)
```

time: 428 us -> 102 us (0.24)
  the two profiles are of different devices: /device:TPU:73 before, /device:TPU:1 now
where the time goes in v1:
time: 102 us
  Pallas kernels  95.6 us (94%)
  local copies, waits for them, and re-layouts  5.45 us (5%)
    pallas_call x1, Pallas kernels, on_device(): pl.pallas_call(functools.partial(kernel, n_row, n_col), out_shape=[jax.Sh...  95.6 us
    unnamed x8, local copies, waits for them, and re-layouts  5.45 us

profile of v1, /device:TPU:1, one launch (start us, length us, event | category | flops | bytes accessed | tf_op | source)
XLA Modules:
  0.0 101.7 jit_solution(5942911274679738021)
XLA Ops:
  0.6 0.0 copy-start
  0.6 1.3 %copy-done = f32[768,384]{1,0:T(8,128)S(1)} copy-done((f32[768,384]{1,0:T(8,128)S(1)}, f32[768,384]{1,0:T(8,128)}, u32[]{:S(2)}) %copy-start) | copy-done | bytes 1179672
  1.9 0.0 copy-start.1
  1.9 1.3 %copy-done.1 = f32[768,384]{1,0:T(8,128)S(1)} copy-done((f32[768,384]{1,0:T(8,128)S(1)}, f32[768,384]{1,0:T(8,128)}, u32[]{:S(2)}) %copy-start.1) | copy-done | bytes 1179672
  3.2 0.0 copy-start.2
  3.2 0.9 copy-done.2
  4.1 95.6 %round.1 = (f32[768,384]{1,0:T(8,128)S(1)}, f32[768,384]{1,0:T(8,128)S(1)}) custom-call(f32[768,384]{1,0:T(8,128)S(1)} %copy-done, f32[768,384]{1,0:T(8,128)S(1)} %copy-done.1, f32[1,24,768]{2,1,0:T(8,128)S(1)} %copy-done.2), custom_call_target="tpu_custom_call" | custom-call | tf_op jit(solution)/shard_map/round/pallas_call | solution.py:247
  99.6 1.0 copy.7
  100.7 1.0 copy.8
Async XLA Ops:
  0.6 1.3 %copy-start = (f32[768,384]{1,0:T(8,128)S(1)}, f32[768,384]{1,0:T(8,128)}, u32[]{:S(2)}) copy-start(f32[768,384]{1,0:T(8,128)} %m_ref.1) | copy-start | bytes 3538948
  1.9 1.3 %copy-start.1 = (f32[768,384]{1,0:T(8,128)S(1)}, f32[768,384]{1,0:T(8,128)}, u32[]{:S(2)}) copy-start(f32[768,384]{1,0:T(8,128)} %v_ref.1) | copy-start | bytes 3538948
  3.2 0.9 copy-start.2

commit v2 on v1

--- a/solution.py
+++ b/solution.py
@@ -49,10 +49,15 @@
     z, l = lax.div(p, 2), lax.rem(p, 2)
     core, lane = (r, c + 1 - 2 * s), (r, c + 2 - 4 * l)
     z_next, z_last = (r, lax.rem(c + 4, n_col)), (r, lax.rem(c + n_col - 4, n_col))
-    half_row = (r + 1 - 2 * h, c)
     y_next, y_last = (lax.rem(r + 2, n_row), c), (lax.rem(r + n_row - 2, n_row), c)
-    across = [(p, 2 * r + t) for t in range(2)]
-    across_self = [(p == r) & (s == t) for t in range(2)]
+
+    def source_z(at):
+        return lax.rem(at - 2 * z + 2 * n_z, n_z)
+
+    across = [(2 * lax.rem(2 * y + z, n_y) + (l if e == 0 else 1 - l), 2 * r + t) for e in range(2) for t in range(2)]
+    across_from = [(p, 4 * source_z(y) + 2 * (h if e == 0 else 1 - h) + t) for e in range(2) for t in range(2)]
+    across_self = [(to[0] == r) & (to[1] == c) for to in across]
+    across_same = [(who[0] == r) & (who[1] == c) for who in across_from]
     col_to, col_from = target(c, n_col), origin(c, n_col)
     row_to = [target(2 * r + u, 2 * n_row) for u in range(2)]
     row_from = [origin(2 * r + u, 2 * n_row) for u in range(2)]
@@ -64,16 +69,16 @@
     m_same = [(m_from[u][0] == r) & (col_from == c) for u in range(2)]
 
     barrier = pltpu.get_barrier_semaphore()
-    awaited = 7
+    awaited = 6
 
     def greet(device):
         pl.semaphore_signal(barrier, inc=1, device_id=device, device_id_type=MESH)
 
-    for device in (core, lane, z_next, z_last, half_row, y_next, y_last):
+    for device in (core, lane, z_next, z_last, y_next, y_last):
         greet(device)
     for same in (*across_self, v_self, *m_self):
         awaited = awaited + jnp.where(same, 0, 1)
-    for device, same in ((across[0], across_self[0]), (across[1], across_self[1]), (v_from, v_self),
+    for device, same in (*zip(across_from, across_same), (v_from, v_self),
                          (m_from[0], m_same[0]), (m_from[1], m_same[1])):
         pl.when(jnp.logical_not(same))(functools.partial(greet, device))
 
@@ -101,83 +106,88 @@
         return copy
 
     crossed = []
-    for t in range(2):
+    for i, device in enumerate(across):
+        t = i % 2
         src = rot_ref.at[0, :, t * width:(t + 1) * width]
         sem = next(index)
-        far = describe(src, rp.at[c], across[t], sem)
+        far = describe(src, rp.at[c], device, sem)
         near = pltpu.make_async_copy(src, rp.at[c], recv_sem.at[sem])
-        pl.when(jnp.logical_not(across_self[t]))(far.start)
-        pl.when(across_self[t])(near.start)
-        crossed.append((far, across_self[t], t, sem))
+        pl.when(jnp.logical_not(across_self[i]))(far.start)
+        pl.when(across_self[i])(near.start)
+        crossed.append((far, across_self[i], sem))
     src = rot_ref.at[0]
-    ring_z = {(0, 1, 0): send(src, rr.at[z, l, s], z_next), (0, -1, 0): send(src, rr.at[z, l, s], z_last)}
+    ring_z = {(0, d, 0): send(src, rr.at[z, l, s], device) for d, device in ((1, z_next), (-1, z_last))}
     to_lane = send(src, rr.at[z, l, s], lane)
     mine = pl.ds(pl.multiple_of(s * width, width), width)
     got_v = send(v_ref, vf.at[:, mine], core)
     got_m = send(m_ref, mf.at[:, mine], core)
-
-    def row_block(who_y, who_h):
-        return rp.at[pl.ds(2 * (2 * who_y + who_h), 2)]
-
-    def chip_block(who_z, who_l):
-        return rr.at[who_z, who_l, s]
-
-    for t in range(2):
-        far, _, _, sem = crossed[t]
-        pl.when(s == t)(lambda sem=sem: pltpu.make_async_copy(
-            rp.at[pl.ds(2 * r, 2)], rp.at[pl.ds(2 * r, 2)], recv_sem.at[sem]).wait())
-    block = row_block(y, h)
-    ring_y = {(0, 1, 0): send(block, block, y_next), (0, -1, 0): send(block, block, y_last)}
-    to_half = send(block, block, half_row)
-
-    to_lane.wait_recv()
-    for d, device in ((1, z_next), (-1, z_last)):
-        ring_z[0, d, 1] = send(chip_block(z, 1 - l), chip_block(z, 1 - l), device)
-    own.wait()
-    both = rr.at[z, :, s]
-    core_z = [send(both, both, core)]
-    to_half.wait_recv()
-    block = row_block(y, 1 - h)
-    for d, device in ((1, y_next), (-1, y_last)):
-        ring_y[0, d, 1] = send(block, block, device)
-
-    def ring(k, size, ring_of, place, pick, ways):
+    ring_y, core_z = {}, []
+
+    def z_block(at, part):
+        return rr.at[at, l if part == 0 else 1 - l, s]
+
+    def y_block(at, part):
+        return rp.at[4 * source_z(at) + 2 * (h if part < 2 else 1 - h) + part % 2]
+
+    def ring(k, size, ring_of, place, pick, device_of, parts, every):
         far = size // 2
-        for lane_of in range(2):
-            for d, device in ways:
-                if (k - 1, d, lane_of) not in ring_of:
-                    continue
-                ring_of[k - 1, d, lane_of].wait_recv()
-                at = lax.rem(place - d * k + size, size)
-                block = pick(at, lane_of)
-                if k < far - 1 or (k == far - 1 and (d == 1) == (lane_of == 0)):
-                    ring_of[k, d, lane_of] = send(block, block, device)
-
-    pick_y = lambda at, lane_of: row_block(at, h if lane_of == 0 else 1 - h)
-    pick_z = lambda at, lane_of: chip_block(at, l if lane_of == 0 else 1 - l)
-    ways_y, ways_z = ((1, y_next), (-1, y_last)), ((1, z_next), (-1, z_last))
-    for k in range(1, max(n_y, n_z) // 2 + 1):
-        if k <= n_y // 2:
-            ring(k, n_y, ring_y, y, pick_y, ways_y)
-        if k <= n_z // 2:
-            ring(k, n_z, ring_z, z, pick_z, ways_z)
+        for part in parts:
+            for d in (1, -1):
+                if k > 0:
+                    if (k - 1, d, part) not in ring_of:
+                        continue
+                    ring_of[k - 1, d, part].wait_recv()
+                block = pick(lax.rem(place - d * k + size, size), part)
+                if k < far - 1 or (k == far - 1 and (d == 1) == (part < every // 2)):
+                    ring_of[k, d, part] = send(block, block, device_of[d])
+
+    def step_z(k, part):
+        ring(k, n_z, ring_z, z, z_block, {1: z_next, -1: z_last}, (part,), 2)
+        if part == 1 and k > 0:
             for d in (1, -1) if k < n_z // 2 else (1,):
                 both = rr.at[lax.rem(z - d * k + n_z, n_z), :, s]
                 core_z.append(send(both, both, core))
+
+    def split_rp(at):
+        high, low = halves(rp[pl.ds(4 * at, 4)].reshape(4 * shard, width))
+        rows = pl.ds(pl.multiple_of(at * (4 * shard), 4 * shard), 4 * shard)
+        rph[rows, :] = high
+        rpl[rows, :] = low
+
+    def step_y(k, side):
+        ring(k, n_y, ring_y, y, y_block, {1: y_next, -1: y_last}, (2 * side, 2 * side + 1), 4)
+        if side == 1:
+            for d in (1, -1) if 0 < k < n_y // 2 else (1,):
+                split_rp(source_z(lax.rem(y - d * k + n_y, n_y)))
+
+    def arrived(e):
+        block = rp.at[pl.ds(4 * source_z(y) + 2 * (h if e == 0 else 1 - h), 2)]
+        for t in range(2):
+            pl.when(s == t)(pltpu.make_async_copy(block, block, recv_sem.at[crossed[2 * e + t][2]]).wait)
+
+    to_lane.wait_recv()
+    step_z(0, 1)
+    own.wait()
+    both = rr.at[z, :, s]
+    core_z.append(send(both, both, core))
+    step_z(1, 0)
+    arrived(0)
+    step_y(0, 0)
+    step_z(1, 1)
+    step_z(2, 0)
+    arrived(1)
+    step_y(0, 1)
+    for k in range(1, n_y // 2 + 1):
+        step_y(k, 0)
+        if k + 1 <= n_z // 2:
+            step_z(k + 1, 1)
+        if k + 2 <= n_z // 2:
+            step_z(k + 2, 0)
+        step_y(k, 1)
     own_v.wait()
     own_m.wait()
     got_v.wait_recv()
     got_m.wait_recv()
-
-    count = n_col // 4
-    rows_of = 4 * shard
-
-    @pl.loop(0, count)
-    def _(i):
-        high, low = halves(rp[pl.ds(4 * i, 4)].reshape(rows_of, width))
-        at = pl.ds(pl.multiple_of(i * rows_of, rows_of), rows_of)
-        rph[at, :] = high
-        rpl[at, :] = low
 
     step = 256 if height % 256 == 0 else height // 3
     v_sem = next(index)
@@ -225,7 +235,7 @@
         pltpu.make_async_copy(part, part, recv_sem.at[m_sem[u]]).wait()
     for copy in sends:
         copy.wait_send()
-    for far, same, _, _ in crossed:
+    for far, same, _ in crossed:
         pl.when(jnp.logical_not(same))(far.wait_send)
     v_out = describe(out_v, ov_ref, v_to, v_sem)
     pl.when(jnp.logical_not(v_self))(v_out.wait_send)
@@ -260,12 +270,12 @@
                 pltpu.VMEM((height, width), BF16),
                 pltpu.VMEM((height, width), F32),
                 pltpu.VMEM((height, width), F32),
-                pltpu.SemaphoreType.DMA((64,)),
-                pltpu.SemaphoreType.DMA((64,)),
+                pltpu.SemaphoreType.DMA((80,)),
+                pltpu.SemaphoreType.DMA((80,)),
                 pltpu.SemaphoreType.DMA((3,)),
             ],
             compiler_params=pltpu.CompilerParams(
-                collective_id=0, has_side_effects=True, vmem_limit_bytes=40 * 1024 * 1024),
+                collective_id=0, has_side_effects=True, vmem_limit_bytes=60 * 1024 * 1024),
             name="round",
         )(matrix, vectors, rotations)
 

time: 102 us -> 97 us (0.951)
  Pallas kernels: 95.6 us -> 92.6 us
  local copies, waits for them, and re-layouts: 5.45 us -> 3.47 us
    pallas_call x1, Pallas kernels: 95.6 us -> 92.6 us  [on_device(): pl.pallas_call(functools.partial(kernel, n_row, n_col), out_shape=[jax.Sh...]
    unnamed x8 -> x4, local copies, waits for them, and re-layouts: 5.45 us -> 3.47 us
where the time goes in v2:
time: 97 us; the launch traced here: 96.7 us
  Pallas kernels  92.6 us (95%)
  local copies, waits for them, and re-layouts  3.47 us (4%)
    pallas_call x1, Pallas kernels, on_device(): pl.pallas_call(functools.partial(kernel, n_row, n_col), out_shape=[jax.Sh...  92.6 us
    unnamed x4, local copies, waits for them, and re-layouts  3.47 us

profile of v2, /device:TPU:1, one launch (start us, length us, event | category | flops | bytes accessed | tf_op | source)
XLA Modules:
  0.0 96.7 jit_solution(13710362095585188258)
XLA Ops:
  0.6 92.6 %round.1 = (f32[768,384]{1,0:T(8,128)}, f32[768,384]{1,0:T(8,128)}) custom-call(f32[768,384]{1,0:T(8,128)} %m_ref.1, f32[768,384]{1,0:T(8,128)} %v_ref.1, f32[1,24,768]{2,1,0:T(8,128)} %rot_ref.1), custom_call_target="tpu_custom_call" | custom-call | tf_op jit(solution)/shard_map/round/pallas_call | solution.py:257
  93.3 0.0 copy-start
  93.3 2.5 %copy.7 = f32[768,384]{1,0:T(8,128)} copy(f32[768,384]{1,0:T(8,128)} %get-tuple-element.4) | data formatting | bytes 2359296
  95.7 0.0 copy-done
  95.7 1.0 %copy.8 = f32[768,384]{1,0:T(8,128)} copy(f32[768,384]{1,0:T(8,128)S(1)} %copy-done) | data formatting | bytes 2359296
Async XLA Ops:
  93.3 2.5 %copy-start = (f32[768,384]{1,0:T(8,128)S(1)}, f32[768,384]{1,0:T(8,128)}, u32[]{:S(2)}) copy-start(f32[768,384]{1,0:T(8,128)} %get-tuple-element.5) | copy-start | bytes 3538948

commit v3 on v2

--- a/solution.py
+++ b/solution.py
@@ -38,7 +38,7 @@
 
 
 def kernel(n_row, n_col, m_ref, v_ref, rot_ref, om_ref, ov_ref, mf, vf, rp, rr, rph, rpl, mrh, mrl,
-           out_v, out_m, send_sem, recv_sem, loc_sem):
+           out_v, out_m, passed, send_sem, recv_sem, loc_sem, pass_send, pass_recv):
     height, width = m_ref.shape
     full = 2 * width
     shard = rot_ref.shape[1]
@@ -68,6 +68,19 @@
     m_self = [(m_to[u][0] == r) & (col_to == c) for u in range(2)]
     m_same = [(m_from[u][0] == r) & (col_from == c) for u in range(2)]
 
+    def among(row):
+        return (row == 1) | (row == n_row - 2)
+
+    edge = (c == 0) | (c == n_col - 2)
+    relayed = [among(m_to[u][0]) & edge & (lax.rem(row_to[u], 2) == 0) for u in range(2)]
+    middle = [(m_to[u][0], jnp.where(c == 0, 2, n_col - 4)) for u in range(2)]
+    relaying = among(r) & ((c == 2) | (c == n_col - 4))
+    relay_from = (m_from[0][0], jnp.where(c == 2, 0, n_col - 2))
+    relay_to = (r, jnp.where(c == 2, 0, n_col - 1))
+    through = among(r) & ((c == 0) | (c == n_col - 1))
+    m_giver = (jnp.where(through, r, m_from[0][0]),
+               jnp.where(through, jnp.where(c == 0, 2, n_col - 4), col_from))
+
     barrier = pltpu.get_barrier_semaphore()
     awaited = 6
 
@@ -79,8 +92,14 @@
     for same in (*across_self, v_self, *m_self):
         awaited = awaited + jnp.where(same, 0, 1)
     for device, same in (*zip(across_from, across_same), (v_from, v_self),
-                         (m_from[0], m_same[0]), (m_from[1], m_same[1])):
+                         (m_giver, m_same[0]), (m_from[1], m_same[1])):
         pl.when(jnp.logical_not(same))(functools.partial(greet, device))
+
+    awaited = awaited + jnp.where(relaying, 1, 0)
+
+    @pl.when(relaying)
+    def _():
+        greet(relay_from)
 
     own = pltpu.make_async_copy(rot_ref.at[0], rr.at[z, l, s], loc_sem.at[0])
     own.start()
@@ -198,11 +217,14 @@
         pl.when(jnp.logical_not(same))(far.start)
         pl.when(same)(pltpu.make_async_copy(src, dst, recv_sem.at[sem]).start)
 
-    @pl.loop(0, height // step)
-    def _(i):
-        at = pl.ds(pl.multiple_of(i * step, step), step)
-        out_v[at, :] = product(halves(vf[at, :]), (rph[...], rpl[...]), (1,))
-        move(out_v.at[at], ov_ref.at[at], v_to, v_self, v_sem)
+    def turn():
+        @pl.loop(0, height // step)
+        def _(i):
+            at = pl.ds(pl.multiple_of(i * step, step), step)
+            out_v[at, :] = product(halves(vf[at, :]), (rph[...], rpl[...]), (1,))
+            move(out_v.at[at], ov_ref.at[at], v_to, v_self, v_sem)
+
+    pl.when(jnp.logical_not(edge))(turn)
 
     @pl.loop(0, height // step)
     def _(i):
@@ -215,6 +237,7 @@
         copy.wait_recv()
 
     tile = 128 if width % 128 == 0 else width
+    pieces = width // tile
     for u in range(2):
         slot = lax.rem(row_to[u], 2)
         dst_base = slot * width
@@ -227,7 +250,31 @@
             at = pl.ds(src_at, tile)
             out_m[at, :] = product(halves(part), (mrh[...], mrl[...]), (0,))
             to = pl.ds(pl.multiple_of(dst_base + i * tile, tile), tile)
-            move(out_m.at[at], om_ref.at[to], m_to[u], m_self[u], sem)
+            pl.when(jnp.logical_not(relayed[u]))(
+                functools.partial(move, out_m.at[at], om_ref.at[to], m_to[u], m_self[u], sem))
+
+            @pl.when(relayed[u])
+            def _():
+                pltpu.make_async_remote_copy(
+                    src_ref=out_m.at[at], dst_ref=passed.at[pl.ds(pl.multiple_of(i * tile, tile), tile)], send_sem=send_sem.at[sem],
+                    recv_sem=pass_recv.at[i], device_id=middle[u], device_id_type=MESH).start()
+
+    pl.when(edge)(turn)
+
+    def passing(i):
+        at = pl.ds(i * tile, tile)
+        return pltpu.make_async_remote_copy(
+            src_ref=passed.at[at], dst_ref=om_ref.at[at], send_sem=pass_send.at[i], recv_sem=recv_sem.at[m_sem[0]],
+            device_id=relay_to, device_id_type=MESH)
+
+    @pl.when(relaying)
+    def _():
+        for i in range(pieces):
+            at = pl.ds(i * tile, tile)
+            pltpu.make_async_copy(passed.at[at], passed.at[at], pass_recv.at[i]).wait()
+            passing(i).start()
+        for i in range(pieces):
+            passing(i).wait_send()
 
     pltpu.make_async_copy(ov_ref, ov_ref, recv_sem.at[v_sem]).wait()
     for u in range(2):
@@ -270,9 +317,12 @@
                 pltpu.VMEM((height, width), BF16),
                 pltpu.VMEM((height, width), F32),
                 pltpu.VMEM((height, width), F32),
+                pltpu.VMEM((width, width), F32),
                 pltpu.SemaphoreType.DMA((80,)),
                 pltpu.SemaphoreType.DMA((80,)),
                 pltpu.SemaphoreType.DMA((3,)),
+                pltpu.SemaphoreType.DMA((width // 128,)),
+                pltpu.SemaphoreType.DMA((width // 128,)),
             ],
             compiler_params=pltpu.CompilerParams(
                 collective_id=0, has_side_effects=True, vmem_limit_bytes=60 * 1024 * 1024),

time: 97 us -> 90.7 us (0.935)
  Pallas kernels: 92.6 us -> 86.4 us
    pallas_call x1, Pallas kernels: 92.6 us -> 86.4 us  [on_device(): pl.pallas_call(functools.partial(kernel, n_row, n_col), out_shape=[jax.Sh...]
where the time goes in v3:
time: 90.7 us; the launch traced here: 90.5 us
  Pallas kernels  86.4 us (95%)
  local copies, waits for them, and re-layouts  3.47 us (4%)
    pallas_call x1, Pallas kernels, on_device(): pl.pallas_call(functools.partial(kernel, n_row, n_col), out_shape=[jax.Sh...  86.4 us
    unnamed x4, local copies, waits for them, and re-layouts  3.47 us

profile of v3, /device:TPU:1, one launch (start us, length us, event | category | flops | bytes accessed | tf_op | source)
XLA Modules:
  0.0 90.5 jit_solution(9220860419016473927)
XLA Ops:
  0.6 86.4 %round.1 = (f32[768,384]{1,0:T(8,128)}, f32[768,384]{1,0:T(8,128)}) custom-call(f32[768,384]{1,0:T(8,128)} %m_ref.1, f32[768,384]{1,0:T(8,128)} %v_ref.1, f32[1,24,768]{2,1,0:T(8,128)} %rot_ref.1), custom_call_target="tpu_custom_call" | custom-call | tf_op jit(solution)/shard_map/round/pallas_call | solution.py:304
  87.0 0.0 copy-start
  87.0 2.5 %copy.7 = f32[768,384]{1,0:T(8,128)} copy(f32[768,384]{1,0:T(8,128)} %get-tuple-element.4) | data formatting | bytes 2359296
  89.5 0.0 copy-done
  89.5 1.0 %copy.8 = f32[768,384]{1,0:T(8,128)} copy(f32[768,384]{1,0:T(8,128)S(1)} %copy-done) | data formatting | bytes 2359296
Async XLA Ops:
  87.0 2.5 %copy-start = (f32[768,384]{1,0:T(8,128)S(1)}, f32[768,384]{1,0:T(8,128)}, u32[]{:S(2)}) copy-start(f32[768,384]{1,0:T(8,128)} %get-tuple-element.5) | copy-start | bytes 3538948

commit v4 on v3

--- a/solution.py
+++ b/solution.py
@@ -54,6 +54,8 @@
     def source_z(at):
         return lax.rem(at - 2 * z + 2 * n_z, n_z)
 
+    y_far = {d: (lax.rem(r + n_row + 4 * d, n_row), c) for d in (1, -1)}
+    z_far = {d: (r, lax.rem(c + n_col + 8 * d, n_col)) for d in (1, -1)}
     across = [(2 * lax.rem(2 * y + z, n_y) + (l if e == 0 else 1 - l), 2 * r + t) for e in range(2) for t in range(2)]
     across_from = [(p, 4 * source_z(y) + 2 * (h if e == 0 else 1 - h) + t) for e in range(2) for t in range(2)]
     across_self = [(to[0] == r) & (to[1] == c) for to in across]
@@ -82,12 +84,12 @@
                jnp.where(through, jnp.where(c == 0, 2, n_col - 4), col_from))
 
     barrier = pltpu.get_barrier_semaphore()
-    awaited = 6
+    awaited = 10
 
     def greet(device):
         pl.semaphore_signal(barrier, inc=1, device_id=device, device_id_type=MESH)
 
-    for device in (core, lane, z_next, z_last, y_next, y_last):
+    for device in (core, lane, z_next, z_last, y_next, y_last, *y_far.values(), *z_far.values()):
         greet(device)
     for same in (*across_self, v_self, *m_self):
         awaited = awaited + jnp.where(same, 0, 1)
@@ -148,7 +150,7 @@
     def y_block(at, part):
         return rp.at[4 * source_z(at) + 2 * (h if part < 2 else 1 - h) + part % 2]
 
-    def ring(k, size, ring_of, place, pick, device_of, parts, every):
+    def ring(k, size, ring_of, place, pick, device_of, far_of, parts, every):
         far = size // 2
         for part in parts:
             for d in (1, -1):
@@ -157,11 +159,13 @@
                         continue
                     ring_of[k - 1, d, part].wait_recv()
                 block = pick(lax.rem(place - d * k + size, size), part)
-                if k < far - 1 or (k == far - 1 and (d == 1) == (part < every // 2)):
+                if k < far - 1:
                     ring_of[k, d, part] = send(block, block, device_of[d])
+                if k == far - 2 and (d == 1) == (part < every // 2):
+                    ring_of[k + 1, d, part] = send(block, block, far_of[d])
 
     def step_z(k, part):
-        ring(k, n_z, ring_z, z, z_block, {1: z_next, -1: z_last}, (part,), 2)
+        ring(k, n_z, ring_z, z, z_block, {1: z_next, -1: z_last}, z_far, (part,), 2)
         if part == 1 and k > 0:
             for d in (1, -1) if k < n_z // 2 else (1,):
                 both = rr.at[lax.rem(z - d * k + n_z, n_z), :, s]
@@ -174,7 +178,7 @@
         rpl[rows, :] = low
 
     def step_y(k, side):
-        ring(k, n_y, ring_y, y, y_block, {1: y_next, -1: y_last}, (2 * side, 2 * side + 1), 4)
+        ring(k, n_y, ring_y, y, y_block, {1: y_next, -1: y_last}, y_far, (2 * side, 2 * side + 1), 4)
         if side == 1:
             for d in (1, -1) if 0 < k < n_y // 2 else (1,):
                 split_rp(source_z(lax.rem(y - d * k + n_y, n_y)))
@@ -294,6 +298,22 @@
         pl.when(jnp.logical_not(m_self[u]))(out.wait_send)
 
 
+def settle(*refs):
+    given, out, (held, came, left) = refs[:2], refs[2:4], refs[4:]
+    parts = came.shape[1]
+    rows = given[0].shape[0] // parts
+    pieces = [(a, i, slice(i * rows, (i + 1) * rows)) for i in range(parts) for a in range(2)]
+    fetch = [pltpu.make_async_copy(given[a].at[at], held.at[a, at], came.at[a, i]) for a, i, at in pieces]
+    store = [pltpu.make_async_copy(held.at[a, at], out[a].at[at], left.at[a, i]) for a, i, at in pieces]
+    for copy in fetch:
+        copy.start()
+    for first, second in zip(fetch, store):
+        first.wait()
+        second.start()
+    for copy in store:
+        copy.wait()
+
+
 def solution(mesh):
     n_row, n_col = mesh.shape["row"], mesh.shape["col"]
 
@@ -301,7 +321,7 @@
         height, width = matrix.shape
         shard = rotations.shape[1]
         any_space = pl.BlockSpec(memory_space=pl.ANY)
-        return pl.pallas_call(
+        moved = pl.pallas_call(
             functools.partial(kernel, n_row, n_col),
             out_shape=[jax.ShapeDtypeStruct((height, width), F32)] * 2,
             in_specs=[any_space] * 3,
@@ -328,6 +348,19 @@
                 collective_id=0, has_side_effects=True, vmem_limit_bytes=60 * 1024 * 1024),
             name="round",
         )(matrix, vectors, rotations)
+        return pl.pallas_call(
+            settle,
+            out_shape=[jax.ShapeDtypeStruct((height, width), F32)] * 2,
+            in_specs=[any_space] * 2,
+            out_specs=[any_space] * 2,
+            scratch_shapes=[
+                pltpu.VMEM((2, height, width), F32),
+                pltpu.SemaphoreType.DMA((2, 4)),
+                pltpu.SemaphoreType.DMA((2, 4)),
+            ],
+            compiler_params=pltpu.CompilerParams(vmem_limit_bytes=60 * 1024 * 1024),
+            name="settle",
+        )(*moved)
 
     return jax.shard_map(
         on_device, mesh=mesh,

time: 90.7 us -> 89.6 us (0.988)
  local copies, waits for them, and re-layouts: 3.47 us -> 0 us
  Pallas kernels: 86.4 us -> 88.7 us
    unnamed x4 -> x0, local copies, waits for them, and re-layouts: 3.47 us -> none
    pallas_call x0 -> x1, Pallas kernels: none -> 2.49 us  [on_device(): pl.pallas_call(settle, out_shape=[jax.ShapeDtypeStruct((height, width), F...]
where the time goes in v4:
time: 89.6 us; the launch traced here: 89.3 us
  Pallas kernels  88.7 us (99%)
    pallas_call x1, Pallas kernels, on_device(): pl.pallas_call(functools.partial(kernel, n_row, n_col), out_shape=[jax.Sh...  86.2 us
    pallas_call x1, Pallas kernels, on_device(): pl.pallas_call(settle, out_shape=[jax.ShapeDtypeStruct((height, width), F...  2.49 us

profile of v4, /device:TPU:1, one launch (start us, length us, event | category | flops | bytes accessed | tf_op | source)
XLA Modules:
  0.0 89.3 jit_solution(9881409828241376729)
XLA Ops:
  0.6 86.2 %round.1 = (f32[768,384]{1,0:T(8,128)}, f32[768,384]{1,0:T(8,128)}) custom-call(f32[768,384]{1,0:T(8,128)} %m_ref.1, f32[768,384]{1,0:T(8,128)} %v_ref.1, f32[1,24,768]{2,1,0:T(8,128)} %rot_ref.1), custom_call_target="tpu_custom_call" | custom-call | tf_op jit(solution)/shard_map/round/pallas_call | solution.py:324
  86.8 2.5 %settle.1 = (f32[768,384]{1,0:T(8,128)}, f32[768,384]{1,0:T(8,128)}) custom-call(f32[768,384]{1,0:T(8,128)} %get-tuple-element.4.refs_0_, f32[768,384]{1,0:T(8,128)} %get-tuple-element.5.refs_1_), custom_call_target="tpu_custom_call" | custom-call | tf_op jit(solution)/shard_map/settle/pallas_call | solution.py:351

commit v5 on v4

--- a/solution.py
+++ b/solution.py
@@ -212,7 +212,7 @@
     got_v.wait_recv()
     got_m.wait_recv()
 
-    step = 256 if height % 256 == 0 else height // 3
+    step = 128 if height % 128 == 0 else height // 3
     v_sem = next(index)
     m_sem = [next(index) for _ in range(2)]
 

time: 89.6 us -> 89.2 us (level)
  no operation moved by 1% of the time
where the time goes in v5:
time: 89.2 us; the launch traced here: 89 us
  Pallas kernels  88.4 us (99%)
    pallas_call x1, Pallas kernels, on_device(): pl.pallas_call(functools.partial(kernel, n_row, n_col), out_shape=[jax.Sh...  85.9 us
    pallas_call x1, Pallas kernels, on_device(): pl.pallas_call(settle, out_shape=[jax.ShapeDtypeStruct((height, width), F...  2.49 us

profile of v5, /device:TPU:1, one launch (start us, length us, event | category | flops | bytes accessed | tf_op | source)
XLA Modules:
  0.0 89.0 jit_solution(14829586176829607790)
XLA Ops:
  0.6 85.9 %round.1 = (f32[768,384]{1,0:T(8,128)}, f32[768,384]{1,0:T(8,128)}) custom-call(f32[768,384]{1,0:T(8,128)} %m_ref.1, f32[768,384]{1,0:T(8,128)} %v_ref.1, f32[1,24,768]{2,1,0:T(8,128)} %rot_ref.1), custom_call_target="tpu_custom_call" | custom-call | tf_op jit(solution)/shard_map/round/pallas_call | solution.py:324
  86.5 2.5 %settle.1 = (f32[768,384]{1,0:T(8,128)}, f32[768,384]{1,0:T(8,128)}) custom-call(f32[768,384]{1,0:T(8,128)} %get-tuple-element.4.refs_0_, f32[768,384]{1,0:T(8,128)} %get-tuple-element.5.refs_1_), custom_call_target="tpu_custom_call" | custom-call | tf_op jit(solution)/shard_map/settle/pallas_call | solution.py:351
